TPU v7x, 512 devices: a whole 4x4x16 slice. The times are simulated.
512 devices in a mesh: ex: 64 (over z, y), layer: 8 (over x, core).
Axes of the slice: x: 4, y: 4, z: 16, core: 2. Of those that a mesh axis runs over, the one named last changes fastest.
Arguments:
- query_acts: bfloat16 [8, 14336, 8192], P('layer', 'ex'), may hold values from -16 to 16
- query_grads: bfloat16 [8, 4096, 8192], P('layer', 'ex'), may hold values from -16 to 16
- proj_in: bfloat16 [8, 64, 14336], P('layer', None, 'ex'), may hold values from -0.046875 to 0.046875
- proj_out: bfloat16 [8, 64, 4096], P('layer', None, 'ex'), may hold values from -0.09375 to 0.09375
- precond_out: float32 [8, 64, 64], P('layer'), may hold values from -0.75 to 0.75
- precond_in: float32 [8, 64, 64], P('layer'), may hold values from -0.75 to 0.75
- train_sketch: bfloat16 [8, 2048, 4096], P('layer', 'ex'), may hold values from -0.5 to 0.5
Outputs:
- scores: float32 [128, 2048], P('layer', 'ex')
All inputs are finite; a program needn't handle non-finite values.
Results may differ from a plain program's by a relative error of at most 0.0029.
Values may be sent and summed in bfloat16 or wider, within the bound.
A program may use at most 64 MiB of HBM per device.

v0:
```python
import jax
import jax.numpy as jnp
from jax import lax
from jax.sharding import PartitionSpec as P

TQ = 64


def on_device(query_acts, query_grads, proj_in, proj_out, precond_out, precond_in, train_sketch):
    rank = proj_in.shape[1]
    first_dims = (((0,), (1,)), ((), ()))
    last_dims = (((1,), (1,)), ((), ()))
    owned_acts = lax.all_to_all(query_acts[0], "ex", split_axis=1, concat_axis=0, tiled=True)
    owned_grads = lax.all_to_all(query_grads[0], "ex", split_axis=1, concat_axis=0, tiled=True)
    full_in = lax.all_gather(proj_in[0], "ex", axis=1, tiled=True)
    full_out = lax.all_gather(proj_out[0], "ex", axis=1, tiled=True)
    proj_acts = lax.dot_general(owned_acts, full_in, first_dims, preferred_element_type=jnp.float32)
    proj_grads = lax.dot_general(
        owned_grads, full_out, first_dims, preferred_element_type=jnp.float32
    )
    own_count = proj_acts.shape[0] // TQ
    proj_acts = proj_acts.reshape(own_count, TQ, rank)
    proj_grads = proj_grads.reshape(own_count, TQ, rank)
    sketch = jnp.einsum("qtr,qts->qrs", proj_grads, proj_acts, precision=lax.Precision.HIGHEST) / TQ
    left = jnp.einsum("ab,qbc->qac", precond_out[0], sketch, precision=lax.Precision.HIGHEST)
    both = jnp.einsum("qac,cd->qad", left, precond_in[0], precision=lax.Precision.HIGHEST)
    precond_sketch = both.astype(jnp.bfloat16).reshape(own_count, rank * rank)
    stored = train_sketch[0]
    partial_value = lax.dot_general(
        lax.all_gather(precond_sketch, "ex", axis=0, tiled=True),
        stored,
        last_dims,
        preferred_element_type=jnp.float32,
    )
    return lax.psum_scatter(partial_value, "layer", scatter_dimension=0, tiled=True)


def solution(mesh):
    placed = (
        P("layer", "ex", None),
        P("layer", "ex", None),
        P("layer", None, "ex"),
        P("layer", None, "ex"),
        P("layer", None, None),
        P("layer", None, None),
        P("layer", "ex", None),
    )
    return jax.shard_map(
        on_device, mesh=mesh, in_specs=placed, out_specs=P("layer", "ex"), check_vma=False
    )
```

profile of v0, /device:TPU:1, one launch (start us, length us, event | category | flops | bytes accessed | tf_op | source)
XLA Modules:
  0.0 574.6 jit_solution(7646979127640157821)
XLA Ops:
  6.5 1.5 copy.31
  8.1 1.7 copy.17
  9.7 19.3 %all-to-all-start = ((bf16[64,64,128]{2,0,1:T(8,128)(2,1)}), bf16[64,64,128]{2,0,1:T(8,128)(2,1)S(1)}, u32[]{:S(2)}, u32[]{:S(2)}) async-start(bf16[64,64,128]{2,0,1:T(8,128)(2,1)} %copy.17), calls=%async_computation | async-start | bytes 2097152 | tf_op jit(solution)/shard_map/all_to_all | solution.py:14
  29.0 3.1 copy.32
  32.1 4.3 copy.21
  36.4 44.1 %all-to-all-done = bf16[64,64,128]{2,0,1:T(8,128)(2,1)S(1)} async-done(((bf16[64,64,128]{2,0,1:T(8,128)(2,1)}), bf16[64,64,128]{2,0,1:T(8,128)(2,1)S(1)}, u32[]{:S(2)}, u32[]{:S(2)}) %all-to-all-start) | async-done | bytes 1048608 | tf_op jit(solution)/shard_map/all_to_all | solution.py:14
  80.5 9.3 %all-to-all-start.1 = ((bf16[224,64,128]{2,0,1:T(8,128)(2,1)}), bf16[224,64,128]{2,0,1:T(8,128)(2,1)}, u32[]{:S(2)}, u32[]{:S(2)}) async-start(bf16[224,64,128]{2,0,1:T(8,128)(2,1)} %copy.21), calls=%async_computation.1 | async-start | bytes 7340032 | tf_op jit(solution)/shard_map/all_to_all | solution.py:13
  89.7 0.0 all-gather.6.cloned.1.call-start
  89.8 0.0 copy-done.2
  89.8 0.8 copy.23
  90.6 0.0 all-gather.6.cloned.1.call-update
  90.6 0.0 all-gather.8.cloned.1.call-start
  90.6 0.1 copy.19
  90.8 252.6 %all-gather = bf16[1,64,4096]{1,0,2:T(2,128)(2,1)S(1)} all-gather(bf16[1,64,64]{1,0,2:T(2,128)(2,1)S(1)} %copy.19), channel_id=2, replica_groups=mesh['ex'=64,'layer'=8] {'ex'}, dimensions={2}, use_global_device_ids=true | all-gather | bytes 532480 | tf_op jit(solution)/shard_map/all_gather | solution.py:16
  343.4 3.6 copy.20
  347.0 14.0 %copy.24 = bf16[1,64,14336]{2,1,0:T(8,128)(2,1)S(1)} copy(bf16[1,64,14336]{1,0,2:T(2,128)(2,1)} %all-gather.6.cloned.1.call-done) | data formatting | bytes 3670016 | tf_op jit(solution)/shard_map/all_gather | solution.py:15
  361.0 1.3 copy.18
  362.3 2.0 fusion.2
  364.3 0.0 all-to-all-done.1
  364.3 6.0 %copy.22 = bf16[128,14336]{1,0:T(8,128)(2,1)} copy(bf16[128,14336]{0,1:T(8,128)(2,1)} %bitcast.8) | data formatting | bytes 7340032 | tf_op jit(solution)/shard_map/dot_general | solution.py:17
  370.3 3.1 fusion
  373.4 0.2 convolution_multiply_fusion
  373.7 0.3 convolution_bitcast_fusion
  374.0 0.3 convolution_convert_fusion
  374.2 0.7 reshape.18
  374.9 0.0 all-gather.8.cloned.1.call-update
  375.0 0.0 reduce-scatter.2.cloned.1.call-start
  375.0 148.3 %all-gather.8.cloned.1.call-done = bf16[64,2,4096]{2,1,0:T(2,128)(2,1)} async-done(((bf16[1,2,4096]{2,1,0:T(2,128)(2,1)}), bf16[64,2,4096]{2,1,0:T(2,128)(2,1)}) %all-gather.8.cloned.1.call-update) | async-done | bytes 1048592 | tf_op jit(solution)/shard_map/all_gather | solution.py:30
  523.4 1.5 reshape.19
  524.8 1.0 fusion.4
  525.9 0.0 reduce-scatter.2.cloned.1.call-update
  525.9 42.1 %reduce-scatter.2.cloned.1.call-done = f32[16,32]{1,0:T(8,128)} async-done(((f32[128,32]{1,0:T(8,128)}), f32[16,32]{1,0:T(8,128)}) %reduce-scatter.2.cloned.1.call-update) | async-done | bytes 2064 | tf_op jit(solution)/shard_map/reduce_scatter | solution.py:35
  (10 shorter events, 0.0 us)
Async XLA Ops:
  6.5 518.3 %copy-start = (bf16[1,32,4096]{2,1,0:T(8,128)(2,1)S(1)}, bf16[1,32,4096]{2,1,0:T(8,128)(2,1)}, u32[]{:S(2)}) copy-start(bf16[1,32,4096]{2,1,0:T(8,128)(2,1)} %param.13) | copy-start | bytes 786436
  9.7 70.7 %all-to-all-start = ((bf16[64,64,128]{2,0,1:T(8,128)(2,1)}), bf16[64,64,128]{2,0,1:T(8,128)(2,1)S(1)}, u32[]{:S(2)}, u32[]{:S(2)}) async-start(bf16[64,64,128]{2,0,1:T(8,128)(2,1)} %copy.17), calls=%async_computation | async-start | bytes 2097152 | tf_op jit(solution)/shard_map/all_to_all | solution.py:14
  36.4 53.4 %copy-start.2 = (bf16[1,64,224]{2,1,0:T(8,128)(2,1)S(1)}, bf16[1,64,224]{2,1,0:T(8,128)(2,1)}, u32[]{:S(2)}) copy-start(bf16[1,64,224]{2,1,0:T(8,128)(2,1)} %param.9) | copy-start | bytes 86020
  36.4 54.3 %copy-start.4 = (bf16[1,64,64]{2,1,0:T(8,128)(2,1)S(1)}, bf16[1,64,64]{2,1,0:T(8,128)(2,1)}, u32[]{:S(2)}) copy-start(bf16[1,64,64]{2,1,0:T(8,128)(2,1)} %param.10) | copy-start | bytes 24580
  80.5 283.8 %all-to-all-start.1 = ((bf16[224,64,128]{2,0,1:T(8,128)(2,1)}), bf16[224,64,128]{2,0,1:T(8,128)(2,1)}, u32[]{:S(2)}, u32[]{:S(2)}) async-start(bf16[224,64,128]{2,0,1:T(8,128)(2,1)} %copy.21), calls=%async_computation.1 | async-start | bytes 7340032 | tf_op jit(solution)/shard_map/all_to_all | solution.py:13
  89.7 257.2 %all-gather.6.cloned.1.call-start = ((), (), s32[]{:S(2)}) async-start(), calls=%async_computation.4 | async-start | bytes 7454720 | tf_op jit(solution)/shard_map/all_gather | solution.py:15
  90.6 432.8 %all-gather.8.cloned.1.call-start = ((), (), s32[]{:S(2)}) async-start(), calls=%async_computation.5 | async-start | bytes 1064960 | tf_op jit(solution)/shard_map/all_gather | solution.py:30
  370.3 3.3 copy-start.1
  370.3 3.6 copy-start.3
  375.0 193.1 %reduce-scatter.2.cloned.1.call-start = ((), (), s32[]{:S(2)}) async-start(), calls=%async_computation.3 | async-start | bytes 73728 | tf_op jit(solution)/shard_map/reduce_scatter | solution.py:35
Sparse Core Ops, SparseCore 0:
  93.5 213.1 all-gather.5
  375.1 148.2 all-gather.7
  526.1 41.8 reduce-scatter.1
where the time goes:
time: 576 us; the launch traced here: 575 us
  blocking collectives  253 us (44%)
  waiting for transfers between devices  235 us (41%)
  local copies, waits for them, and re-layouts  38.5 us (7%)
  starting transfers between devices  28.7 us (5%)
  between operations  13.3 us (2%)
  matrix products  6.9 us (1%)
    all_gather x1, blocking collectives, on_device(): full_out = lax.all_gather(proj_out[0], 'ex', axis=1, tiled=True)  253 us
    all_gather x1, waiting for transfers between devices, on_device(): lax.all_gather(precond_sketch, 'ex', axis=0, tiled=True)  148 us
    all_to_all x1, waiting for transfers between devices, on_device(): lax.all_to_all(query_grads[0], 'ex', split_axis=1, concat_axis=0, tiled=T...  44.1 us
    reduce_scatter x1, waiting for transfers between devices, on_device(): lax.psum_scatter(partial_value, 'layer', scatter_dimension=0, tiled=True)  42.1 us
    all_to_all x1, starting transfers between devices, on_device(): lax.all_to_all(query_grads[0], 'ex', split_axis=1, concat_axis=0, tiled=T...  19.3 us
    all_gather x1, local copies, waits for them, and re-layouts, on_device(): full_in = lax.all_gather(proj_in[0], 'ex', axis=1, tiled=True)  14 us
  transfers between devices with their start and end apart: 5, of which 3 were waited for; matrix products, arithmetic and copies ran while one was open for 5% of the time, Pallas kernels for 0%

commit v1 on v0

--- a/solution.py
+++ b/solution.py
@@ -8,19 +8,15 @@
 
 def on_device(query_acts, query_grads, proj_in, proj_out, precond_out, precond_in, train_sketch):
     rank = proj_in.shape[1]
-    first_dims = (((0,), (1,)), ((), ()))
+    plain = (((1,), (0,)), ((), ()))
     last_dims = (((1,), (1,)), ((), ()))
-    owned_acts = lax.all_to_all(query_acts[0], "ex", split_axis=1, concat_axis=0, tiled=True)
-    owned_grads = lax.all_to_all(query_grads[0], "ex", split_axis=1, concat_axis=0, tiled=True)
-    full_in = lax.all_gather(proj_in[0], "ex", axis=1, tiled=True)
-    full_out = lax.all_gather(proj_out[0], "ex", axis=1, tiled=True)
-    proj_acts = lax.dot_general(owned_acts, full_in, first_dims, preferred_element_type=jnp.float32)
-    proj_grads = lax.dot_general(
-        owned_grads, full_out, first_dims, preferred_element_type=jnp.float32
-    )
-    own_count = proj_acts.shape[0] // TQ
-    proj_acts = proj_acts.reshape(own_count, TQ, rank)
-    proj_grads = proj_grads.reshape(own_count, TQ, rank)
+    part_acts = lax.dot_general(proj_in[0], query_acts[0], plain, preferred_element_type=jnp.float32)
+    part_grads = lax.dot_general(proj_out[0], query_grads[0], plain, preferred_element_type=jnp.float32)
+    both_parts = jnp.concatenate([part_acts, part_grads], axis=0)
+    summed = lax.psum_scatter(both_parts, "ex", scatter_dimension=1, tiled=True)
+    own_count = summed.shape[1] // TQ
+    proj_acts = summed[:rank].T.reshape(own_count, TQ, rank)
+    proj_grads = summed[rank:].T.reshape(own_count, TQ, rank)
     sketch = jnp.einsum("qtr,qts->qrs", proj_grads, proj_acts, precision=lax.Precision.HIGHEST) / TQ
     left = jnp.einsum("ab,qbc->qac", precond_out[0], sketch, precision=lax.Precision.HIGHEST)
     both = jnp.einsum("qac,cd->qad", left, precond_in[0], precision=lax.Precision.HIGHEST)

time: 576 us -> 900 us (1.56)
  waiting for transfers between devices: 235 us -> 875 us
  blocking collectives: 253 us -> 0 us
  local copies, waits for them, and re-layouts: 38.5 us -> 3.15 us
  starting transfers between devices: 28.7 us -> 0.09 us
    reduce_scatter x0 -> x1, waiting for transfers between devices: none -> 694 us  [on_device(): summed = lax.psum_scatter(both_parts, 'ex', scatter_dimension=1, tiled=True)]
    all_gather x1 -> x0, blocking collectives: 253 us -> none  [on_device(): full_out = lax.all_gather(proj_out[0], 'ex', axis=1, tiled=True)]
    all_to_all x2 -> x0, waiting for transfers between devices: 44.1 us -> none  [the longest x1 44.1 us: on_device(): lax.all_to_all(query_grads[0], 'ex', split_axis=1, concat_axis=0, tiled=T...]
    all_to_all x2 -> x0, starting transfers between devices: 28.5 us -> none  [the longest x1 19.3 us: on_device(): lax.all_to_all(query_grads[0], 'ex', split_axis=1, concat_axis=0, tiled=T...]
    all_gather x2 -> x0, local copies, waits for them, and re-layouts: 17.6 us -> none  [the longest x1 14 us: on_device(): full_in = lax.all_gather(proj_in[0], 'ex', axis=1, tiled=True)]
    all_gather x1, waiting for transfers between devices: 148 us -> 139 us  [on_device(): lax.all_gather(precond_sketch, 'ex', axis=0, tiled=True)]
  transfers between devices with their start and end apart: 5 -> 3, of which waited for: 3 -> 3; matrix products, arithmetic and copies ran while one was open for 5% -> 0% of each run, Pallas kernels for 0% -> 0%
where the time goes in v1:
time: 900 us; the launch traced here: 899 us
  waiting for transfers between devices  875 us (97%)
  between operations  13.2 us (1%)
    reduce_scatter x1, waiting for transfers between devices, on_device(): summed = lax.psum_scatter(both_parts, 'ex', scatter_dimension=1, tiled=True)  694 us
    all_gather x1, waiting for transfers between devices, on_device(): lax.all_gather(precond_sketch, 'ex', axis=0, tiled=True)  139 us
    reduce_scatter x1, waiting for transfers between devices, on_device(): lax.psum_scatter(partial_value, 'layer', scatter_dimension=0, tiled=True)  42.3 us
  transfers between devices with their start and end apart: 3, of which 3 were waited for; matrix products, arithmetic and copies ran while one was open for 0% of the time, Pallas kernels for 0%

profile of v1, /device:TPU:1, one launch (start us, length us, event | category | flops | bytes accessed | tf_op | source)
XLA Modules:
  0.0 898.8 jit_solution(12774469874132605078)
XLA Ops:
  6.5 0.0 copy-start
  6.5 0.0 copy-start.4
  6.5 0.0 reduce-scatter.3.cloned.1.call-start
  6.5 2.9 fusion
  9.5 0.0 copy-done
  9.5 0.0 copy-done.4
  9.5 0.4 fusion.2
  9.9 2.3 pad_maximum_fusion
  12.2 0.0 copy-start.2
  12.2 0.0 copy-start.3
  12.2 0.0 copy-start.1
  12.2 0.0 reduce-scatter.3.cloned.1.call-update
  12.3 0.0 all-gather.3.cloned.1.call-start
  12.3 694.0 %reduce-scatter.3.cloned.1.call-done = f32[128,128]{1,0:T(8,128)} async-done(((f32[128,8192]{1,0:T(8,128)}), f32[128,128]{1,0:T(8,128)}) %reduce-scatter.3.cloned.1.call-update) | async-done | bytes 65552 | tf_op jit(solution)/shard_map/reduce_scatter | solution.py:16
  706.3 0.8 slice_bitcast_fusion.1
  707.1 0.1 reshape.9
  707.2 0.1 copy.10
  707.3 0.2 convolution_multiply_fusion
  707.5 0.0 copy-done.2
  707.5 0.2 convolution_bitcast_fusion
  707.7 0.0 copy-done.3
  707.7 0.2 convolution_convert_fusion
  707.9 0.7 reshape.12
  708.6 0.0 all-gather.3.cloned.1.call-update
  708.6 0.0 reduce-scatter.5.cloned.1.call-start
  708.7 138.7 %all-gather.3.cloned.1.call-done = bf16[64,2,4096]{2,1,0:T(2,128)(2,1)} async-done(((bf16[1,2,4096]{2,1,0:T(2,128)(2,1)}), bf16[64,2,4096]{2,1,0:T(2,128)(2,1)}) %all-gather.3.cloned.1.call-update) | async-done | bytes 1048592 | tf_op jit(solution)/shard_map/all_gather | solution.py:26
  847.4 1.5 reshape.13
  848.8 0.0 copy-done.1
  848.9 1.0 fusion.4
  849.9 0.0 reduce-scatter.5.cloned.1.call-update
  849.9 42.3 %reduce-scatter.5.cloned.1.call-done = f32[16,32]{1,0:T(8,128)} async-done(((f32[128,32]{1,0:T(8,128)}), f32[16,32]{1,0:T(8,128)}) %reduce-scatter.5.cloned.1.call-update) | async-done | bytes 2064 | tf_op jit(solution)/shard_map/reduce_scatter | solution.py:31
Async XLA Ops:
  6.5 2.9 copy-start
  6.5 2.9 copy-start.4
  6.5 699.8 %reduce-scatter.3.cloned.1.call-start = ((), (), s32[]{:S(2)}) async-start(), calls=%async_computation.2 | async-start | bytes 4259840 | tf_op jit(solution)/shard_map/reduce_scatter | solution.py:16
  12.2 695.3 %copy-start.2 = (f32[1,64,64]{2,1,0:T(8,128)S(1)}, f32[1,64,64]{2,1,0:T(8,128)}, u32[]{:S(2)}) copy-start(f32[1,64,64]{2,1,0:T(8,128)} %param.11) | copy-start | bytes 49156
  12.2 695.5 %copy-start.3 = (f32[1,64,64]{2,1,0:T(8,128)S(1)}, f32[1,64,64]{2,1,0:T(8,128)}, u32[]{:S(2)}) copy-start(f32[1,64,64]{2,1,0:T(8,128)} %param.12) | copy-start | bytes 49156
  12.2 836.6 %copy-start.1 = (bf16[1,32,4096]{2,1,0:T(8,128)(2,1)S(1)}, bf16[1,32,4096]{2,1,0:T(8,128)(2,1)}, u32[]{:S(2)}) copy-start(bf16[1,32,4096]{2,1,0:T(8,128)(2,1)} %param.13) | copy-start | bytes 786436
  12.3 835.1 %all-gather.3.cloned.1.call-start = ((), (), s32[]{:S(2)}) async-start(), calls=%async_computation.4 | async-start | bytes 1064960 | tf_op jit(solution)/shard_map/all_gather | solution.py:26
  708.6 183.6 %reduce-scatter.5.cloned.1.call-start = ((), (), s32[]{:S(2)}) async-start(), calls=%async_computation.3 | async-start | bytes 73728 | tf_op jit(solution)/shard_map/reduce_scatter | solution.py:31
Sparse Core Ops, SparseCore 0:
  12.4 693.8 reduce-scatter.2
  709.7 137.6 all-gather.2
  850.4 41.8 reduce-scatter.4

commit v2 on v1

v2 whole, which is shorter than its diff:
```python
import functools

import jax
import jax.numpy as jnp
from jax import lax
from jax.experimental import pallas as pl
from jax.experimental.pallas import tpu as pltpu
from jax.sharding import PartitionSpec as P

NY = 4
R = 64
T = 128
K = 80.0
LAG1 = 2
LAG2 = 4
AGLAG = 3
MESH = pl.DeviceIdType.MESH
NT = (((1,), (1,)), ((), ()))


def encode(x):
    top = jnp.max(jnp.abs(x), axis=0, keepdims=True)
    scale = jnp.maximum(top * 1.01, 1e-36).astype(jnp.bfloat16).astype(jnp.float32)
    return jnp.exp(x * (K / scale)).astype(jnp.bfloat16), scale


def decode(code, scale):
    return jnp.log(code.astype(jnp.float32)) * (scale * (1.0 / K))


def put(ref, pieces):
    rows = 16 // len(pieces)
    scales = []
    for n, piece in enumerate(pieces):
        code, scale = encode(piece)
        ref[R * n : R * (n + 1), :] = code
        scales.append(jnp.broadcast_to(scale, (rows, T)))
    tile = scales[0] if len(scales) == 1 else jnp.concatenate(scales, axis=0)
    ref[R * len(pieces) : R * len(pieces) + 16, :] = tile.astype(jnp.bfloat16)


def get(ref, count):
    rows = 16 // count
    scales = ref[R * count : R * count + 16, :].astype(jnp.float32)
    return [
        decode(ref[R * n : R * (n + 1), :], scales[rows * n : rows * n + 1, :])
        for n in range(count)
    ]


def kernel(
    nz, nl,
    acts, grads, pin, pout, pco, pci, train, out,
    xa, xg, pa, pg, total, h1s, h1r, h2s, h2r, zs, zr, ag, xf, tr, wide, pi2, part, lr,
    sxa, sxg, str_, h1ss, h1rs, h2ss, h2rs, zss, zrs, azs, azr, y1s, y1r, y2s, y2r, lss, lrs,
):
    ne = nz * NY
    half = nz // 2
    ex = lax.axis_index("ex")
    layer = lax.axis_index("layer")
    z = ex // NY
    y = ex % NY
    up, down = (y + 1) % NY, (y + NY - 1) % NY
    across = (y + 2) % NY

    def at(zz, yy):
        return (zz * NY + yy, layer)

    y_up, y_down = at(z, up), at(z, down)

    def column(j):
        offset = jnp.where(j % 2 == 1, half - (j + 1) // 2, j // 2 - half)
        return (z + offset + nz) % nz

    def load(j):
        columns = pl.ds(pl.multiple_of(column(j) * (NY * T), NY * T), NY * T)
        return (
            pltpu.make_async_copy(acts.at[0, :, columns], xa.at[j], sxa.at[j]),
            pltpu.make_async_copy(grads.at[0, :, columns], xg.at[j], sxg.at[j]),
        )

    def start_load(j, _):
        for copy in load(j):
            copy.start()
        return 0

    lax.fori_loop(0, nz, start_load, 0)
    load_train = pltpu.make_async_copy(train.at[0], tr, str_)
    load_train.start()

    barrier = pltpu.get_barrier_semaphore()
    greeted = [y_up, y_down]
    greeted += [at((z + step + nz) % nz, y) for step in (1, -1, 2, -2)]
    greeted += [(ex, (layer + step) % nl) for step in range(1, nl)]
    for device in greeted:
        pl.semaphore_signal(barrier, inc=1, device_id=device, device_id_type=MESH)

    def remote(src, dst, ssem, rsem, device):
        return pltpu.make_async_remote_copy(
            src_ref=src, dst_ref=dst, send_sem=ssem, recv_sem=rsem,
            device_id=device, device_id_type=MESH,
        )

    def hop1(j, way):
        return remote(h1s.at[j, way], h1r.at[j, way], h1ss, h1rs.at[j, way], (y_up, y_down)[way])

    def hop2(j, way):
        return remote(h2s.at[j, way], h2r.at[j, way], h2ss, h2rs.at[j, way], (y_up, y_down)[way])

    def zstep(j):
        step = jnp.where((j == 0) | (j % 2 == 1), 1, -1)
        later = jnp.where(j == 0, 1, j + 2)
        return remote(zs.at[j], zr.at[later], zss, zrs.at[later], at((z + step + nz) % nz, y))

    def zwait(slot):
        remote(zs.at[0], zr.at[slot], zss, zrs.at[slot], at((z + 1) % nz, y)).wait_recv()

    def project(j):
        for copy in load(j):
            copy.wait()
        a = jnp.dot(pin[0], xa[j], preferred_element_type=jnp.float32)
        g = jnp.dot(pout[0], xg[j], preferred_element_type=jnp.float32)
        for d in range(NY):
            pa[j, d] = a[:, d * T : (d + 1) * T]
            pg[j, d] = g[:, d * T : (d + 1) * T]
        put(h1s.at[j, 0], [pa[j, across], pg[j, up]])
        put(h1s.at[j, 1], [pg[j, across], pa[j, down]])

        @pl.when(j == 0)
        def _():
            pl.semaphore_wait(barrier, len(greeted))

        hop1(j, 0).start()
        hop1(j, 1).start()

    def pass_on(j):
        hop1(j, 0).wait_recv()
        a_on, g_here = get(h1r.at[j, 0], 2)
        put(h2s.at[j, 0], [a_on + pa[j, up]])
        hop2(j, 0).start()
        hop1(j, 1).wait_recv()
        g_on, a_here = get(h1r.at[j, 1], 2)
        put(h2s.at[j, 1], [g_on + pg[j, down]])
        hop2(j, 1).start()
        total[j, 0] = a_here + pa[j, y]
        total[j, 1] = g_here + pg[j, y]

    def finish_y(j):
        hop2(j, 0).wait_recv()
        hop2(j, 1).wait_recv()
        (a,) = get(h2r.at[j, 0], 1)
        (g,) = get(h2r.at[j, 1], 1)
        return total[j, 0] + a, total[j, 1] + g

    def along_z(j):
        a, g = finish_y(j)
        met = (j == 1) | (j >= 3)

        @pl.when(met)
        def _():
            zwait(j)
            a_in, g_in = get(zr.at[j], 2)
            put(zs.at[j], [a + a_in, g + g_in])

        @pl.when(jnp.logical_not(met))
        def _():
            put(zs.at[j], [a, g])

        zstep(j).start()

    def turn(i, _):
        @pl.when(i < nz)
        def _():
            project(i)

        @pl.when((i >= LAG1) & (i < nz + LAG1))
        def _():
            pass_on(i - LAG1)

        @pl.when(i >= LAG2)
        def _():
            along_z(i - LAG2)

        return 0

    lax.fori_loop(0, nz - 1 + LAG2, turn, 0)

    two = jnp.concatenate([pci[0], pci[0]], axis=1)
    two = jnp.concatenate([two, two], axis=0)
    row_low = lax.broadcasted_iota(jnp.int32, (T, T), 0) < R
    lane_low = lax.broadcasted_iota(jnp.int32, (T, T), 1) < R
    pi2[...] = jnp.where(row_low == lane_low, two, 0.0)

    a, g = finish_y(nz - 1)
    for slot in (nz - 1, nz):
        zwait(slot)
        a_in, g_in = get(zr.at[slot], 2)
        a = a + a_in
        g = g + g_in
    a2 = jnp.where(row_low == lane_low, jnp.concatenate([a, a], axis=0), 0.0)
    high = lax.Precision.HIGHEST
    sketch = lax.dot_general(g, a2, NT, precision=high, preferred_element_type=jnp.float32)
    sketch = sketch * (1.0 / 64)
    left = jnp.dot(pco[0], sketch, precision=high, preferred_element_type=jnp.float32)
    both = jnp.dot(left, pi2[...], precision=high, preferred_element_type=jnp.float32)
    own = both.astype(jnp.bfloat16)
    ag[ex] = own

    def spread(e, values):
        xf[pl.ds(e, R, stride=ne), :] = values.astype(jnp.float32)

    def away(t):
        d = (t + 1) // 2
        return (z + jnp.where(t % 2 == 1, -d, d) + nz) % nz

    def gz(t, later, step):
        e = away(t) * NY + y
        return remote(ag.at[e], ag.at[e], azs, azr.at[later], at((z + step + nz) % nz, y))

    def gy1(t, way):
        e = away(t) * NY + y
        return remote(ag.at[e], ag.at[e], y1s, y1r.at[t, way], (y_up, y_down)[way])

    def gy1_wait(t, way):
        e = away(t) * NY + (down, up)[way]
        remote(ag.at[e], ag.at[e], y1s, y1r.at[t, way], (y_up, y_down)[way]).wait_recv()
        return e

    def gy2(t, way):
        e = away(t) * NY + (down, up)[way]
        rows = pl.ds(way * (R // 2), R // 2)
        return remote(
            ag.at[e, rows], ag.at[e, rows], y2s, y2r.at[t, way], (y_up, y_down)[way]
        )

    def gy2_wait(t):
        e = away(t) * NY + across
        for way in range(2):
            rows = pl.ds(way * (R // 2), R // 2)
            remote(
                ag.at[e, rows], ag.at[e, rows], y2s, y2r.at[t, way], (y_up, y_down)[way]
            ).wait_recv()
        return e

    gz(0, 1, 1).start()
    gz(0, 2, -1).start()
    gz(0, 3, 2).start()
    if nz > 4:
        gz(0, 4, -2).start()
    gy1(0, 0).start()
    gy1(0, 1).start()
    spread(ex, own)

    load_train.wait()
    lanes = lax.broadcasted_iota(jnp.int32, (tr.shape[0], T), 1) < R

    def widen(j, _):
        tile = tr[:, pl.ds(pl.multiple_of(j * T, T), T)].astype(jnp.float32)
        turned = pltpu.roll(tile, R, 1)
        first = jnp.concatenate(
            [jnp.where(lanes, tile, 0.0), jnp.where(lanes, turned, 0.0)], axis=1
        )
        second = jnp.concatenate(
            [jnp.where(lanes, 0.0, turned), jnp.where(lanes, 0.0, tile)], axis=1
        )
        full = jnp.concatenate([first, second, jnp.zeros((T - R, 2 * T), jnp.float32)], axis=0)
        wide[j] = full.astype(jnp.bfloat16)
        return 0

    lax.fori_loop(0, R // 2, widen, 0)

    remote(h1s, h1r, h1ss, h1rs.at[0, 0], y_up).wait_send()
    remote(h2s, h2r, h2ss, h2rs.at[0, 0], y_up).wait_send()
    remote(zs, zr.at[0 : nz - 1], zss, zrs.at[0], y_up).wait_send()

    def gather(t, _):
        @pl.when((t > 0) & (t < nz))
        def _():
            gz(t, t, 1).wait_recv()
            d = (t + 1) // 2
            step = jnp.where(t % 2 == 1, 1, -1)

            @pl.when((d % 2 == 0) & (t + 2 < nz))
            def _():
                gz(t, t + 2, step).start()

            @pl.when((d % 2 == 0) & (t + 4 < nz))
            def _():
                gz(t, t + 4, 2 * step).start()

            gy1(t, 0).start()
            gy1(t, 1).start()
            e = away(t) * NY + y
            spread(e, ag[e])

        @pl.when((t >= AGLAG) & (t < nz + AGLAG))
        def _():
            u = t - AGLAG
            e0 = gy1_wait(u, 0)
            gy2(u, 0).start()
            e1 = gy1_wait(u, 1)
            gy2(u, 1).start()
            spread(e0, ag[e0])
            spread(e1, ag[e1])

        @pl.when(t >= 2 * AGLAG)
        def _():
            e = gy2_wait(t - 2 * AGLAG)
            spread(e, ag[e])

        return 0

    lax.fori_loop(0, nz + 2 * AGLAG, gather, 0)

    def score(j, acc):
        x0 = xf[pl.ds(pl.multiple_of(2 * j * ne, 8), ne), :]
        x1 = xf[pl.ds(pl.multiple_of((2 * j + 1) * ne, 8), ne), :]
        x = jnp.concatenate([x0, x1], axis=1).astype(jnp.bfloat16)
        return acc + lax.dot_general(x, wide[j], NT, preferred_element_type=jnp.float32)

    part[...] = lax.fori_loop(
        0, R // 2, score, jnp.zeros((ne, T), jnp.float32), unroll=8
    )

    rows = ne // nl

    def layer_copy(step):
        target = (layer + step) % nl
        block = pl.ds(pl.multiple_of(target * rows, 8), rows)
        return remote(part.at[block], lr.at[step - 1], lss, lrs.at[step - 1], (ex, target))

    for step in range(1, nl):
        layer_copy(step).start()
    remote(ag.at[0 : nz - 1], ag.at[0 : nz - 1], azs, azr.at[0], y_up).wait_send()
    remote(ag.at[0 : 2 * nz], ag.at[0 : 2 * nz], y1s, y1r.at[0, 0], y_up).wait_send()
    remote(ag.at[0:nz], ag.at[0:nz], y2s, y2r.at[0, 0], y_up).wait_send()
    result = part[pl.ds(pl.multiple_of(layer * rows, 8), rows), :]
    for step in range(1, nl):
        layer_copy(step).wait_recv()
        result = result + lr[step - 1]
    out[...] = result
    remote(lr, lr, lss, lrs.at[0], y_up).wait_send()


def on_device(nz, nl, query_acts, query_grads, proj_in, proj_out, precond_out, precond_in, train_sketch):
    ff, d = query_acts.shape[1], query_grads.shape[1]
    examples = train_sketch.shape[1]
    ne = nz * NY
    rows = ne // nl
    bf16, f32 = jnp.bfloat16, jnp.float32
    dma = pltpu.SemaphoreType.DMA
    vmem = pl.BlockSpec(memory_space=pltpu.VMEM)
    hbm = pl.BlockSpec(memory_space=pl.ANY)
    summed = pl.pallas_call(
        functools.partial(kernel, nz, nl),
        out_shape=jax.ShapeDtypeStruct((rows, T), f32),
        in_specs=[hbm, hbm, vmem, vmem, vmem, vmem, hbm],
        out_specs=vmem,
        scratch_shapes=[
            pltpu.VMEM((nz, ff, NY * T), bf16),
            pltpu.VMEM((nz, d, NY * T), bf16),
            pltpu.VMEM((nz, NY, R, T), f32),
            pltpu.VMEM((nz, NY, R, T), f32),
            pltpu.VMEM((nz, 2, R, T), f32),
            pltpu.VMEM((nz, 2, 2 * R + 16, T), bf16),
            pltpu.VMEM((nz, 2, 2 * R + 16, T), bf16),
            pltpu.VMEM((nz, 2, R + 16, T), bf16),
            pltpu.VMEM((nz, 2, R + 16, T), bf16),
            pltpu.VMEM((nz - 1, 2 * R + 16, T), bf16),
            pltpu.VMEM((nz + 1, 2 * R + 16, T), bf16),
            pltpu.VMEM((ne, R, T), bf16),
            pltpu.VMEM((R * ne, T), f32),
            pltpu.VMEM((examples, R * R), bf16),
            pltpu.VMEM((R // 2, T, 2 * T), bf16),
            pltpu.VMEM((T, T), f32),
            pltpu.VMEM((ne, T), f32),
            pltpu.VMEM((nl - 1, rows, T), f32),
            dma((nz,)), dma((nz,)), dma,
            dma, dma((nz, 2)), dma, dma((nz, 2)),
            dma, dma((nz + 1,)),
            dma, dma((nz,)), dma, dma((nz, 2)), dma, dma((nz, 2)),
            dma, dma((nl - 1,)),
        ],
        compiler_params=pltpu.CompilerParams(
            collective_id=0, has_side_effects=True, vmem_limit_bytes=48 * 2**20
        ),
    )(query_acts, query_grads, proj_in, proj_out, precond_out, precond_in, train_sketch)
    return summed[:, : 2 * examples].reshape(2 * rows, examples)


def solution(mesh):
    nz, nl = mesh.shape["ex"] // NY, mesh.shape["layer"]
    placed = (
        P("layer", "ex", None),
        P("layer", "ex", None),
        P("layer", None, "ex"),
        P("layer", None, "ex"),
        P("layer", None, None),
        P("layer", None, None),
        P("layer", "ex", None),
    )
    return jax.shard_map(
        functools.partial(on_device, nz, nl),
        mesh=mesh, in_specs=placed, out_specs=P("layer", "ex"), check_vma=False,
    )
```

time: 900 us -> 88.4 us (0.10)
  waiting for transfers between devices: 875 us -> 0 us
  Pallas kernels: 0 us -> 80 us
  between operations: 13.2 us -> 0.02 us
    reduce_scatter x2 -> x0, waiting for transfers between devices: 736 us -> none  [the longest x1 694 us: on_device(): summed = lax.psum_scatter(both_parts, 'ex', scatter_dimension=1, tiled=True)]
    all_gather x1 -> x0, waiting for transfers between devices: 139 us -> none  [on_device(): lax.all_gather(precond_sketch, 'ex', axis=0, tiled=True)]
    pallas_call x0 -> x1, Pallas kernels: none -> 80 us  [on_device(): pl.pallas_call(functools.partial(kernel, nz, nl), out_shape=jax.ShapeDtyp...]
  transfers between devices with their start and end apart: 3 -> 0, of which waited for: 3 -> 0; matrix products, arithmetic and copies ran while one was open for 0% -> 0% of each run, Pallas kernels for 0% -> 0%
where the time goes in v2:
time: 88.4 us; the launch traced here: 87.9 us
  Pallas kernels  80 us (90%)
  local copies, waits for them, and re-layouts  7.87 us (9%)
    pallas_call x1, Pallas kernels, on_device(): pl.pallas_call(functools.partial(kernel, nz, nl), out_shape=jax.ShapeDtyp...  80 us
    unnamed x14, local copies, waits for them, and re-layouts  7.2 us

profile of v2, /device:TPU:1, one launch (start us, length us, event | category | flops | bytes accessed | tf_op | source)
XLA Modules:
  0.0 87.9 jit_solution(14139398606913757248)
XLA Ops:
  0.0 0.0 copy-start
  0.0 2.0 %copy-done = bf16[1,224,8192]{2,1,0:T(8,128)(2,1)S(1)} copy-done((bf16[1,224,8192]{2,1,0:T(8,128)(2,1)S(1)}, bf16[1,224,8192]{2,1,0:T(8,128)(2,1)}, u32[]{:S(2)}) %copy-start) | copy-done | bytes 3670040
  2.0 0.0 copy-start.1
  2.0 1.2 %copy-done.1 = bf16[1,64,8192]{2,1,0:T(8,128)(2,1)S(1)} copy-done((bf16[1,64,8192]{2,1,0:T(8,128)(2,1)S(1)}, bf16[1,64,8192]{2,1,0:T(8,128)(2,1)}, u32[]{:S(2)}) %copy-start.1) | copy-done | bytes 1048600
  3.3 0.0 copy-start.2
  3.3 0.9 %copy-done.2 = bf16[1,32,4096]{2,1,0:T(8,128)(2,1)S(1)} copy-done((bf16[1,32,4096]{2,1,0:T(8,128)(2,1)S(1)}, bf16[1,32,4096]{2,1,0:T(8,128)(2,1)}, u32[]{:S(2)}) %copy-start.2) | copy-done | bytes 262168
  4.2 0.0 copy-start.3
  4.2 0.8 copy-done.3
  5.0 0.0 copy-start.4
  5.0 0.8 copy-done.4
  5.7 0.0 copy-start.5
  5.7 0.8 copy-done.5
  6.5 0.0 copy-start.6
  6.5 0.7 copy-done.6
  7.2 80.0 %shard_map.73 = f32[8,128]{1,0:T(8,128)S(1)} custom-call(bf16[1,224,8192]{2,1,0:T(8,128)(2,1)S(1)} %copy-done, bf16[1,64,8192]{2,1,0:T(8,128)(2,1)S(1)} %copy-done.1, bf16[1,64,224]{2,1,0:T(8,128)(2,1)S(1)} %copy-done.3, bf16[1,64,64]{2,1,0:T(8,128)(2,1)S(1)} %copy-done.6, f32[1,64,64]{2,1,0:T(8,128)S(1)} %copy-done.4, f32[1,64,64]{2,1,0:T(8,128)S(1)} %copy-done.5, ...), custom_call_target="tpu_custom_call" | custom-call | tf_op jit(solution)/shard_map/pallas_call | solution.py:354
  87.3 0.7 reshape.3
Async XLA Ops:
  0.0 2.0 %copy-start = (bf16[1,224,8192]{2,1,0:T(8,128)(2,1)S(1)}, bf16[1,224,8192]{2,1,0:T(8,128)(2,1)}, u32[]{:S(2)}) copy-start(bf16[1,224,8192]{2,1,0:T(8,128)(2,1)} %acts.1) | copy-start | bytes 11010052
  2.0 1.2 %copy-start.1 = (bf16[1,64,8192]{2,1,0:T(8,128)(2,1)S(1)}, bf16[1,64,8192]{2,1,0:T(8,128)(2,1)}, u32[]{:S(2)}) copy-start(bf16[1,64,8192]{2,1,0:T(8,128)(2,1)} %grads.1) | copy-start | bytes 3145732
  3.3 0.9 %copy-start.2 = (bf16[1,32,4096]{2,1,0:T(8,128)(2,1)S(1)}, bf16[1,32,4096]{2,1,0:T(8,128)(2,1)}, u32[]{:S(2)}) copy-start(bf16[1,32,4096]{2,1,0:T(8,128)(2,1)} %train.1) | copy-start | bytes 786436
  4.2 0.8 copy-start.3
  5.0 0.8 copy-start.4
  5.7 0.8 copy-start.5
  6.5 0.7 copy-start.6

commit v3 on v2

--- a/solution.py
+++ b/solution.py
@@ -11,9 +11,8 @@
 R = 64
 T = 128
 K = 80.0
-LAG1 = 2
-LAG2 = 4
-AGLAG = 3
+LAG1 = 3
+LAG2 = 6
 MESH = pl.DeviceIdType.MESH
 NT = (((1,), (1,)), ((), ()))
 
@@ -50,12 +49,13 @@
 
 def kernel(
     nz, nl,
-    acts, grads, pin, pout, pco, pci, train, out,
-    xa, xg, pa, pg, total, h1s, h1r, h2s, h2r, zs, zr, ag, xf, tr, wide, pi2, part, lr,
-    sxa, sxg, str_, h1ss, h1rs, h2ss, h2rs, zss, zrs, azs, azr, y1s, y1r, y2s, y2r, lss, lrs,
+    acts, grads, pin_in, pout_in, pco_in, pci_in, train, out,
+    pin, pout, pco, pci, xa, xg, pa, pg, total, h1s, h1r, h2s, h2r, zs, zr, ag, xf, tr, wide, pi2, part, lr,
+    sw, sxa, sxg, str_, h1ss, h1rs, h2ss, h2rs, zss, zrs, azs, azr, y1s, y1r, y2s, y2r, lss, lrs,
 ):
     ne = nz * NY
     half = nz // 2
+    hub = half // 2
     ex = lax.axis_index("ex")
     layer = lax.axis_index("layer")
     z = ex // NY
@@ -84,7 +84,17 @@
             copy.start()
         return 0
 
+    small = [
+        pltpu.make_async_copy(src, dst, sw.at[n])
+        for n, (src, dst) in enumerate(
+            [(pin_in, pin), (pout_in, pout), (pco_in, pco), (pci_in, pci)]
+        )
+    ]
+    for copy in small[:2]:
+        copy.start()
     lax.fori_loop(0, nz, start_load, 0)
+    for copy in small[2:]:
+        copy.start()
     load_train = pltpu.make_async_copy(train.at[0], tr, str_)
     load_train.start()
 
@@ -108,12 +118,16 @@
         return remote(h2s.at[j, way], h2r.at[j, way], h2ss, h2rs.at[j, way], (y_up, y_down)[way])
 
     def zstep(j):
-        step = jnp.where((j == 0) | (j % 2 == 1), 1, -1)
-        later = jnp.where(j == 0, 1, j + 2)
-        return remote(zs.at[j], zr.at[later], zss, zrs.at[later], at((z + step + nz) % nz, y))
-
-    def zwait(slot):
-        remote(zs.at[0], zr.at[slot], zss, zrs.at[slot], at((z + 1) % nz, y)).wait_recv()
+        h = (nz - j) // 2
+        way = jnp.where((j == 0) | (j % 2 == 1), 1, -1)
+        far = 1 - h % 2
+        later = jnp.where(j == 0, 3, j + 2 + 2 * far)
+        there = (z + way * (1 + far) + nz) % nz
+        return remote(zs.at[j], zr.at[later, far], zss, zrs.at[later, far], at(there, y))
+
+    def zget(slot, far):
+        remote(zs.at[0], zr.at[slot, far], zss, zrs.at[slot, far], y_up).wait_recv()
+        return get(zr.at[slot, far], 2)
 
     def project(j):
         for copy in load(j):
@@ -154,19 +168,37 @@
 
     def along_z(j):
         a, g = finish_y(j)
-        met = (j == 1) | (j >= 3)
-
-        @pl.when(met)
-        def _():
-            zwait(j)
-            a_in, g_in = get(zr.at[j], 2)
-            put(zs.at[j], [a + a_in, g + g_in])
-
-        @pl.when(jnp.logical_not(met))
-        def _():
-            put(zs.at[j], [a, g])
-
+        total[j, 0] = a
+        total[j, 1] = g
+        h = (nz - j) // 2
+
+        @pl.when((h % 2 == 0) & (j > 0))
+        def _():
+            a_in, g_in = zget(j, 0)
+            total[j, 0] += a_in
+            total[j, 1] += g_in
+
+            @pl.when((h < half - 2) | (j % 2 == 1))
+            def _():
+                a_in, g_in = zget(j, 1)
+                total[j, 0] += a_in
+                total[j, 1] += g_in
+
+        put(zs.at[j], [total[j, 0], total[j, 1]])
         zstep(j).start()
+
+    lanes = lax.broadcasted_iota(jnp.int32, (tr.shape[0], T), 1) < R
+
+    def widen(j):
+        tile = tr[:, pl.ds(pl.multiple_of(j * T, T), T)].astype(jnp.float32)
+        turned = pltpu.roll(tile, R, 1)
+        first = jnp.concatenate(
+            [jnp.where(lanes, tile, 0.0), jnp.where(lanes, turned, 0.0)], axis=1
+        )
+        second = jnp.concatenate(
+            [jnp.where(lanes, 0.0, turned), jnp.where(lanes, 0.0, tile)], axis=1
+        )
+        wide[j] = jnp.concatenate([first, second], axis=0).astype(jnp.bfloat16)
 
     def turn(i, _):
         @pl.when(i < nz)
@@ -181,8 +213,16 @@
         def _():
             along_z(i - LAG2)
 
-        return 0
-
+        @pl.when(i < nz)
+        def _():
+            for n in range(R // 2 // nz):
+                widen(i * (R // 2 // nz) + n)
+
+        return 0
+
+    for copy in small:
+        copy.wait()
+    load_train.wait()
     lax.fori_loop(0, nz - 1 + LAG2, turn, 0)
 
     two = jnp.concatenate([pci[0], pci[0]], axis=1)
@@ -192,9 +232,8 @@
     pi2[...] = jnp.where(row_low == lane_low, two, 0.0)
 
     a, g = finish_y(nz - 1)
-    for slot in (nz - 1, nz):
-        zwait(slot)
-        a_in, g_in = get(zr.at[slot], 2)
+    for slot, far in ((nz - 1, 0), (nz, 0), (nz - 1, 1), (nz, 1)):
+        a_in, g_in = zget(slot, far)
         a = a + a_in
         g = g + g_in
     a2 = jnp.where(row_low == lane_low, jnp.concatenate([a, a], axis=0), 0.0)
@@ -242,75 +281,97 @@
             ).wait_recv()
         return e
 
-    gz(0, 1, 1).start()
-    gz(0, 2, -1).start()
-    gz(0, 3, 2).start()
-    if nz > 4:
-        gz(0, 4, -2).start()
+    for d in [hub, hub + 1] + list(range(hub - 1, 0, -1)):
+        gz(0, 2 * d - 1, d).start()
+        gz(0, 2 * d, -d).start()
     gy1(0, 0).start()
     gy1(0, 1).start()
-    spread(ex, own)
-
-    load_train.wait()
-    lanes = lax.broadcasted_iota(jnp.int32, (tr.shape[0], T), 1) < R
-
-    def widen(j, _):
-        tile = tr[:, pl.ds(pl.multiple_of(j * T, T), T)].astype(jnp.float32)
-        turned = pltpu.roll(tile, R, 1)
-        first = jnp.concatenate(
-            [jnp.where(lanes, tile, 0.0), jnp.where(lanes, turned, 0.0)], axis=1
-        )
-        second = jnp.concatenate(
-            [jnp.where(lanes, 0.0, turned), jnp.where(lanes, 0.0, tile)], axis=1
-        )
-        full = jnp.concatenate([first, second, jnp.zeros((T - R, 2 * T), jnp.float32)], axis=0)
-        wide[j] = full.astype(jnp.bfloat16)
-        return 0
-
-    lax.fori_loop(0, R // 2, widen, 0)
+
 
     remote(h1s, h1r, h1ss, h1rs.at[0, 0], y_up).wait_send()
     remote(h2s, h2r, h2ss, h2rs.at[0, 0], y_up).wait_send()
-    remote(zs, zr.at[0 : nz - 1], zss, zrs.at[0], y_up).wait_send()
-
-    def gather(t, _):
-        @pl.when((t > 0) & (t < nz))
-        def _():
-            gz(t, t, 1).wait_recv()
-            d = (t + 1) // 2
-            step = jnp.where(t % 2 == 1, 1, -1)
-
-            @pl.when((d % 2 == 0) & (t + 2 < nz))
-            def _():
-                gz(t, t + 2, step).start()
-
-            @pl.when((d % 2 == 0) & (t + 4 < nz))
-            def _():
-                gz(t, t + 4, 2 * step).start()
-
-            gy1(t, 0).start()
-            gy1(t, 1).start()
-            e = away(t) * NY + y
+    remote(zs, zr.at[0 : nz - 1, 0], zss, zrs.at[0, 0], y_up).wait_send()
+
+    first = 2 * (hub + 1) + 1
+
+    def chunk(n):
+        pair, side = (n - 1) // 2, (n - 1) % 2
+        early = 2 * jnp.where(pair < hub, hub - pair, hub + 1) - 1 + side
+        m = n - first - 1
+        late = jnp.where(n == first, nz - 1, nz - 3 - 2 * (m // 2) + (m + 2) % 2)
+        return jnp.where(n == 0, 0, jnp.where(n < first, early, late))
+
+    def arrived(t):
+        gz(t, t, 1).wait_recv()
+
+    arrived(2 * hub - 1)
+    for d in range(half, hub + 1, -1):
+        gz(2 * hub - 1, 2 * d - 1, d - hub).start()
+    arrived(2 * hub)
+    for d in range(half - 1, hub + 1, -1):
+        gz(2 * hub, 2 * d, hub - d).start()
+
+    def forward(n, _):
+        t = chunk(n)
+
+        @pl.when(n > 2)
+        def _():
+            arrived(t)
+
+        gy1(t, 0).start()
+        gy1(t, 1).start()
+        return 0
+
+    def forward_half(n, _):
+        t = chunk(n)
+        gy1_wait(t, 0)
+        gy2(t, 0).start()
+        gy1_wait(t, 1)
+        gy2(t, 1).start()
+        return 0
+
+    def gy3(t, yy):
+        e = away(t) * NY + yy
+        return remote(ag.at[e], ag.at[e], y2s, y2r.at[t, 0], at(z, across))
+
+    def forward_late(n, _):
+        t = chunk(n)
+        arrived(t)
+        gy3(t, y).start()
+        gy1(t, 0).start()
+        gy1(t, 1).start()
+        return 0
+
+    def spread_three(n, _):
+        t = chunk(n)
+        for yy in (y, down, up):
+            e = away(t) * NY + yy
             spread(e, ag[e])
-
-        @pl.when((t >= AGLAG) & (t < nz + AGLAG))
-        def _():
-            u = t - AGLAG
-            e0 = gy1_wait(u, 0)
-            gy2(u, 0).start()
-            e1 = gy1_wait(u, 1)
-            gy2(u, 1).start()
-            spread(e0, ag[e0])
-            spread(e1, ag[e1])
-
-        @pl.when(t >= 2 * AGLAG)
-        def _():
-            e = gy2_wait(t - 2 * AGLAG)
+        return 0
+
+    def spread_last(n, _):
+        e = gy2_wait(chunk(n))
+        spread(e, ag[e])
+        return 0
+
+    def spread_late(n, _):
+        t = chunk(n)
+        e = away(t) * NY + y
+        spread(e, ag[e])
+        for way in range(2):
+            e = gy1_wait(t, way)
             spread(e, ag[e])
-
-        return 0
-
-    lax.fori_loop(0, nz + 2 * AGLAG, gather, 0)
+        gy3(t, across).wait_recv()
+        e = away(t) * NY + across
+        spread(e, ag[e])
+        return 0
+
+    lax.fori_loop(1, first, forward, 0)
+    lax.fori_loop(0, first, forward_half, 0)
+    lax.fori_loop(first, nz, forward_late, 0)
+    lax.fori_loop(0, first, spread_three, 0)
+    lax.fori_loop(0, first, spread_last, 0)
+    lax.fori_loop(first, nz, spread_late, 0)
 
     def score(j, acc):
         x0 = xf[pl.ds(pl.multiple_of(2 * j * ne, 8), ne), :]
@@ -318,9 +379,9 @@
         x = jnp.concatenate([x0, x1], axis=1).astype(jnp.bfloat16)
         return acc + lax.dot_general(x, wide[j], NT, preferred_element_type=jnp.float32)
 
-    part[...] = lax.fori_loop(
-        0, R // 2, score, jnp.zeros((ne, T), jnp.float32), unroll=8
-    )
+    count = wide.shape[1]
+    scores = lax.fori_loop(0, R // 2, score, jnp.zeros((ne, count), jnp.float32), unroll=8)
+    part[...] = jnp.concatenate([scores, jnp.zeros((ne, T - count), jnp.float32)], axis=1)
 
     rows = ne // nl
 
@@ -354,9 +415,13 @@
     summed = pl.pallas_call(
         functools.partial(kernel, nz, nl),
         out_shape=jax.ShapeDtypeStruct((rows, T), f32),
-        in_specs=[hbm, hbm, vmem, vmem, vmem, vmem, hbm],
+        in_specs=[hbm] * 7,
         out_specs=vmem,
         scratch_shapes=[
+            pltpu.VMEM(proj_in.shape, bf16),
+            pltpu.VMEM(proj_out.shape, bf16),
+            pltpu.VMEM(precond_out.shape, f32),
+            pltpu.VMEM(precond_in.shape, f32),
             pltpu.VMEM((nz, ff, NY * T), bf16),
             pltpu.VMEM((nz, d, NY * T), bf16),
             pltpu.VMEM((nz, NY, R, T), f32),
@@ -367,22 +432,22 @@
             pltpu.VMEM((nz, 2, R + 16, T), bf16),
             pltpu.VMEM((nz, 2, R + 16, T), bf16),
             pltpu.VMEM((nz - 1, 2 * R + 16, T), bf16),
-            pltpu.VMEM((nz + 1, 2 * R + 16, T), bf16),
+            pltpu.VMEM((nz + 1, 2, 2 * R + 16, T), bf16),
             pltpu.VMEM((ne, R, T), bf16),
             pltpu.VMEM((R * ne, T), f32),
             pltpu.VMEM((examples, R * R), bf16),
-            pltpu.VMEM((R // 2, T, 2 * T), bf16),
+            pltpu.VMEM((R // 2, 2 * examples, 2 * T), bf16),
             pltpu.VMEM((T, T), f32),
             pltpu.VMEM((ne, T), f32),
             pltpu.VMEM((nl - 1, rows, T), f32),
-            dma((nz,)), dma((nz,)), dma,
+            dma((4,)), dma((nz,)), dma((nz,)), dma,
             dma, dma((nz, 2)), dma, dma((nz, 2)),
-            dma, dma((nz + 1,)),
+            dma, dma((nz + 1, 2)),
             dma, dma((nz,)), dma, dma((nz, 2)), dma, dma((nz, 2)),
             dma, dma((nl - 1,)),
         ],
         compiler_params=pltpu.CompilerParams(
-            collective_id=0, has_side_effects=True, vmem_limit_bytes=48 * 2**20
+            collective_id=0, has_side_effects=True, vmem_limit_bytes=60 * 2**20
         ),
     )(query_acts, query_grads, proj_in, proj_out, precond_out, precond_in, train_sketch)
     return summed[:, : 2 * examples].reshape(2 * rows, examples)

time: 88.4 us -> 70 us (0.79)
  Pallas kernels: 80 us -> 68.5 us
  local copies, waits for them, and re-layouts: 7.87 us -> 1.35 us
    pallas_call x1, Pallas kernels: 80 us -> 68.5 us  [on_device(): pl.pallas_call(functools.partial(kernel, nz, nl), out_shape=jax.ShapeDtyp...]
    unnamed x14 -> x0, local copies, waits for them, and re-layouts: 7.2 us -> none
where the time goes in v3:
time: 70 us; the launch traced here: 69.9 us
  Pallas kernels  68.5 us (98%)
  local copies, waits for them, and re-layouts  1.35 us (2%)
    pallas_call x1, Pallas kernels, on_device(): pl.pallas_call(functools.partial(kernel, nz, nl), out_shape=jax.ShapeDtyp...  68.5 us

profile of v3, /device:TPU:1, one launch (start us, length us, event | category | flops | bytes accessed | tf_op | source)
XLA Modules:
  0.0 69.9 jit_solution(5593768455850552841)
XLA Ops:
  0.0 68.5 %shard_map.73 = f32[8,128]{1,0:T(8,128)} custom-call(bf16[1,224,8192]{2,1,0:T(8,128)(2,1)} %acts.1, bf16[1,64,8192]{2,1,0:T(8,128)(2,1)} %grads.1, bf16[1,64,224]{2,1,0:T(8,128)(2,1)} %pin_in.1, bf16[1,64,64]{2,1,0:T(8,128)(2,1)} %pout_in.1, f32[1,64,64]{2,1,0:T(8,128)} %pco_in.1, f32[1,64,64]{2,1,0:T(8,128)} %pci_in.1, bf16[1,32,4096]{2,1,0:T(8,128)(2,1)} %train.1), custom_call_target="tpu_custom_call" | custom-call | tf_op jit(solution)/shard_map/pallas_call | solution.py:415
  68.5 1.3 %reshape.3 = f32[16,32]{1,0:T(8,128)} reshape(f32[8,64]{1,0:T(8,128)} %bitcast.1) | data formatting | bytes 4096 | tf_op jit(solution)/shard_map/reshape | solution.py:453

commit v4 on v3

--- a/solution.py
+++ b/solution.py
@@ -12,7 +12,9 @@
 T = 128
 K = 80.0
 LAG1 = 3
+WIDEN = 4
 LAG2 = 6
+ND = 1
 MESH = pl.DeviceIdType.MESH
 NT = (((1,), (1,)), ((), ()))
 
@@ -28,21 +30,21 @@
 
 
 def put(ref, pieces):
-    rows = 16 // len(pieces)
-    scales = []
+    row = lax.broadcasted_iota(jnp.int32, (16, T), 0)
+    span = 16 // len(pieces)
+    tile = jnp.zeros((16, T), jnp.float32)
     for n, piece in enumerate(pieces):
         code, scale = encode(piece)
         ref[R * n : R * (n + 1), :] = code
-        scales.append(jnp.broadcast_to(scale, (rows, T)))
-    tile = scales[0] if len(scales) == 1 else jnp.concatenate(scales, axis=0)
+        tile = jnp.where(row < span * n, tile, scale)
     ref[R * len(pieces) : R * len(pieces) + 16, :] = tile.astype(jnp.bfloat16)
 
 
 def get(ref, count):
-    rows = 16 // count
+    span = 16 // count
     scales = ref[R * count : R * count + 16, :].astype(jnp.float32)
     return [
-        decode(ref[R * n : R * (n + 1), :], scales[rows * n : rows * n + 1, :])
+        decode(ref[R * n : R * (n + 1), :], scales[span * n : span * n + 1, :])
         for n in range(count)
     ]
 
@@ -50,8 +52,8 @@
 def kernel(
     nz, nl,
     acts, grads, pin_in, pout_in, pco_in, pci_in, train, out,
-    pin, pout, pco, pci, xa, xg, pa, pg, total, h1s, h1r, h2s, h2r, zs, zr, ag, xf, tr, wide, pi2, part, lr,
-    sw, sxa, sxg, str_, h1ss, h1rs, h2ss, h2rs, zss, zrs, azs, azr, y1s, y1r, y2s, y2r, lss, lrs,
+    pin, pout, pco, pci, xa, xg, pa, pg, total, h1s, h1r, h2s, h2r, ds, dr, fs, fr, zs, zr, ag, xf, tr, wide, pi2, part, lr,
+    sw, sxa, sxg, str_, h1ss, h1rs, h2ss, h2rs, dss, drs, fss, frs, zss, zrs, azs, azr, y1s, y1r, y2s, y2r, lss, lrs,
 ):
     ne = nz * NY
     half = nz // 2
@@ -99,7 +101,7 @@
     load_train.start()
 
     barrier = pltpu.get_barrier_semaphore()
-    greeted = [y_up, y_down]
+    greeted = [y_up, y_down, at(z, across)]
     greeted += [at((z + step + nz) % nz, y) for step in (1, -1, 2, -2)]
     greeted += [(ex, (layer + step) % nl) for step in range(1, nl)]
     for device in greeted:
@@ -125,27 +127,57 @@
         there = (z + way * (1 + far) + nz) % nz
         return remote(zs.at[j], zr.at[later, far], zss, zrs.at[later, far], at(there, y))
 
+    last = nz - 3
+
+    def straight(j):
+        target = at(z, across)
+        n = j - (last + 1 - ND)
+        return remote(ds.at[n], dr.at[n], dss, drs.at[n], target)
+
+    def neighbour(side):
+        there = at((z + (1, -1)[side] + nz) % nz, y)
+        return remote(fs.at[side], fr.at[side], fss, frs.at[side], there)
+
     def zget(slot, far):
         remote(zs.at[0], zr.at[slot, far], zss, zrs.at[slot, far], y_up).wait_recv()
         return get(zr.at[slot, far], 2)
 
-    def project(j):
-        for copy in load(j):
+    def project(j, place):
+        for copy in load(place):
             copy.wait()
-        a = jnp.dot(pin[0], xa[j], preferred_element_type=jnp.float32)
-        g = jnp.dot(pout[0], xg[j], preferred_element_type=jnp.float32)
+        a = jnp.dot(pin[0], xa[place], preferred_element_type=jnp.float32)
+        g = jnp.dot(pout[0], xg[place], preferred_element_type=jnp.float32)
         for d in range(NY):
             pa[j, d] = a[:, d * T : (d + 1) * T]
             pg[j, d] = g[:, d * T : (d + 1) * T]
+
+    def first_hop(j):
         put(h1s.at[j, 0], [pa[j, across], pg[j, up]])
         put(h1s.at[j, 1], [pg[j, across], pa[j, down]])
 
-        @pl.when(j == 0)
-        def _():
-            pl.semaphore_wait(barrier, len(greeted))
-
+    def send_first_hop(j):
         hop1(j, 0).start()
         hop1(j, 1).start()
+
+    def send_straight(j):
+        put(ds.at[j - (last + 1 - ND)], [pa[j, across], pg[j, across]])
+        straight(j).start()
+        put(h1s.at[j, 0], [pa[j, up], pg[j, up]])
+        hop1(j, 0).start()
+        put(h1s.at[j, 1], [pa[j, down], pg[j, down]])
+        hop1(j, 1).start()
+
+    def to_neighbour(side):
+        place = nz - 3 + side
+        project(place, place)
+        put(fs.at[side], [p[place, d] for d in range(NY) for p in (pa, pg)])
+
+    def from_neighbour(side):
+        neighbour(side).wait_recv()
+        pieces = get(fr.at[side], 2 * NY)
+        for d in range(NY):
+            pa[last, d] += pieces[2 * d]
+            pg[last, d] += pieces[2 * d + 1]
 
     def pass_on(j):
         hop1(j, 0).wait_recv()
@@ -164,12 +196,28 @@
         hop2(j, 1).wait_recv()
         (a,) = get(h2r.at[j, 0], 1)
         (g,) = get(h2r.at[j, 1], 1)
-        return total[j, 0] + a, total[j, 1] + g
+        total[j, 0] += a
+        total[j, 1] += g
+
+    def finish_straight(j):
+        hop1(j, 0).wait_recv()
+        a0, g0 = get(h1r.at[j, 0], 2)
+        hop1(j, 1).wait_recv()
+        a1, g1 = get(h1r.at[j, 1], 2)
+        straight(j).wait_recv()
+        a2, g2 = get(dr.at[j - (last + 1 - ND)], 2)
+        total[j, 0] = a0 + a1 + a2 + pa[j, y]
+        total[j, 1] = g0 + g1 + g2 + pg[j, y]
 
     def along_z(j):
-        a, g = finish_y(j)
-        total[j, 0] = a
-        total[j, 1] = g
+        @pl.when(j <= last - ND)
+        def _():
+            finish_y(j)
+
+        @pl.when(j > last - ND)
+        def _():
+            finish_straight(j)
+
         h = (nz - j) // 2
 
         @pl.when((h % 2 == 0) & (j > 0))
@@ -201,11 +249,27 @@
         wide[j] = jnp.concatenate([first, second], axis=0).astype(jnp.bfloat16)
 
     def turn(i, _):
-        @pl.when(i < nz)
-        def _():
-            project(i)
-
-        @pl.when((i >= LAG1) & (i < nz + LAG1))
+        @pl.when((i > 0) & (i < last))
+        def _():
+            project(i, i)
+
+        @pl.when((i > 0) & (i <= last - ND))
+        def _():
+            first_hop(i)
+            send_first_hop(i)
+
+        @pl.when((i > last - ND) & (i < last))
+        def _():
+            send_straight(i)
+
+        @pl.when(i == last)
+        def _():
+            project(last, nz - 1)
+            from_neighbour(0)
+            from_neighbour(1)
+            send_straight(last)
+
+        @pl.when((i >= LAG1) & (i <= last - ND + LAG1))
         def _():
             pass_on(i - LAG1)
 
@@ -213,17 +277,25 @@
         def _():
             along_z(i - LAG2)
 
-        @pl.when(i < nz)
-        def _():
-            for n in range(R // 2 // nz):
-                widen(i * (R // 2 // nz) + n)
+        @pl.when(i < WIDEN)
+        def _():
+            for n in range(R // 2 // WIDEN):
+                widen(i * (R // 2 // WIDEN) + n)
 
         return 0
 
     for copy in small:
         copy.wait()
+    project(0, 0)
+    first_hop(0)
+    to_neighbour(0)
+    to_neighbour(1)
+    pl.semaphore_wait(barrier, len(greeted))
+    send_first_hop(0)
+    neighbour(0).start()
+    neighbour(1).start()
     load_train.wait()
-    lax.fori_loop(0, nz - 1 + LAG2, turn, 0)
+    lax.fori_loop(0, last + LAG2, turn, 0)
 
     two = jnp.concatenate([pci[0], pci[0]], axis=1)
     two = jnp.concatenate([two, two], axis=0)
@@ -231,9 +303,10 @@
     lane_low = lax.broadcasted_iota(jnp.int32, (T, T), 1) < R
     pi2[...] = jnp.where(row_low == lane_low, two, 0.0)
 
-    a, g = finish_y(nz - 1)
-    for slot, far in ((nz - 1, 0), (nz, 0), (nz - 1, 1), (nz, 1)):
-        a_in, g_in = zget(slot, far)
+    finish_straight(last)
+    a, g = total[last, 0], total[last, 1]
+    for slot in (nz - 1, nz):
+        a_in, g_in = zget(slot, 1)
         a = a + a_in
         g = g + g_in
     a2 = jnp.where(row_low == lane_low, jnp.concatenate([a, a], axis=0), 0.0)
@@ -288,9 +361,8 @@
     gy1(0, 1).start()
 
 
-    remote(h1s, h1r, h1ss, h1rs.at[0, 0], y_up).wait_send()
-    remote(h2s, h2r, h2ss, h2rs.at[0, 0], y_up).wait_send()
-    remote(zs, zr.at[0 : nz - 1, 0], zss, zrs.at[0, 0], y_up).wait_send()
+    for sent, sem in ((h1s, h1ss), (h2s, h2ss), (ds, dss), (fs, fss), (zs, zss)):
+        remote(sent, sent, sem, azr.at[0], y_up).wait_send()
 
     first = 2 * (hub + 1) + 1
 
@@ -427,11 +499,15 @@
             pltpu.VMEM((nz, NY, R, T), f32),
             pltpu.VMEM((nz, NY, R, T), f32),
             pltpu.VMEM((nz, 2, R, T), f32),
-            pltpu.VMEM((nz, 2, 2 * R + 16, T), bf16),
-            pltpu.VMEM((nz, 2, 2 * R + 16, T), bf16),
-            pltpu.VMEM((nz, 2, R + 16, T), bf16),
-            pltpu.VMEM((nz, 2, R + 16, T), bf16),
-            pltpu.VMEM((nz - 1, 2 * R + 16, T), bf16),
+            pltpu.VMEM((nz - 2, 2, 2 * R + 16, T), bf16),
+            pltpu.VMEM((nz - 2, 2, 2 * R + 16, T), bf16),
+            pltpu.VMEM((nz - 2 - ND, 2, R + 16, T), bf16),
+            pltpu.VMEM((nz - 2 - ND, 2, R + 16, T), bf16),
+            pltpu.VMEM((ND, 2 * R + 16, T), bf16),
+            pltpu.VMEM((ND, 2 * R + 16, T), bf16),
+            pltpu.VMEM((2, 2 * NY * R + 16, T), bf16),
+            pltpu.VMEM((2, 2 * NY * R + 16, T), bf16),
+            pltpu.VMEM((nz - 3, 2 * R + 16, T), bf16),
             pltpu.VMEM((nz + 1, 2, 2 * R + 16, T), bf16),
             pltpu.VMEM((ne, R, T), bf16),
             pltpu.VMEM((R * ne, T), f32),
@@ -441,7 +517,7 @@
             pltpu.VMEM((ne, T), f32),
             pltpu.VMEM((nl - 1, rows, T), f32),
             dma((4,)), dma((nz,)), dma((nz,)), dma,
-            dma, dma((nz, 2)), dma, dma((nz, 2)),
+            dma, dma((nz, 2)), dma, dma((nz, 2)), dma, dma((ND,)), dma, dma((2,)),
             dma, dma((nz + 1, 2)),
             dma, dma((nz,)), dma, dma((nz, 2)), dma, dma((nz, 2)),
             dma, dma((nl - 1,)),

time: 70 us -> 68.5 us (0.979)
  Pallas kernels: 68.5 us -> 67 us
    pallas_call x1, Pallas kernels: 68.5 us -> 67 us  [on_device(): pl.pallas_call(functools.partial(kernel, nz, nl), out_shape=jax.ShapeDtyp...]
where the time goes in v4:
time: 68.5 us; the launch traced here: 68.3 us
  Pallas kernels  67 us (98%)
  local copies, waits for them, and re-layouts  1.35 us (2%)
    pallas_call x1, Pallas kernels, on_device(): pl.pallas_call(functools.partial(kernel, nz, nl), out_shape=jax.ShapeDtyp...  67 us

profile of v4, /device:TPU:1, one launch (start us, length us, event | category | flops | bytes accessed | tf_op | source)
XLA Modules:
  0.0 68.3 jit_solution(4795981751662762666)
XLA Ops:
  0.0 67.0 %shard_map.73 = f32[8,128]{1,0:T(8,128)} custom-call(bf16[1,224,8192]{2,1,0:T(8,128)(2,1)} %acts.1, bf16[1,64,8192]{2,1,0:T(8,128)(2,1)} %grads.1, bf16[1,64,224]{2,1,0:T(8,128)(2,1)} %pin_in.1, bf16[1,64,64]{2,1,0:T(8,128)(2,1)} %pout_in.1, f32[1,64,64]{2,1,0:T(8,128)} %pco_in.1, f32[1,64,64]{2,1,0:T(8,128)} %pci_in.1, bf16[1,32,4096]{2,1,0:T(8,128)(2,1)} %train.1), custom_call_target="tpu_custom_call" | custom-call | tf_op jit(solution)/shard_map/pallas_call | solution.py:487
  67.0 1.3 %reshape.3 = f32[16,32]{1,0:T(8,128)} reshape(f32[8,64]{1,0:T(8,128)} %bitcast.1) | data formatting | bytes 4096 | tf_op jit(solution)/shard_map/reshape | solution.py:529

commit v5 on v4

--- a/solution.py
+++ b/solution.py
@@ -15,6 +15,7 @@
 WIDEN = 4
 LAG2 = 6
 ND = 1
+XD = 1
 MESH = pl.DeviceIdType.MESH
 NT = (((1,), (1,)), ((), ()))
 
@@ -53,7 +54,7 @@
     nz, nl,
     acts, grads, pin_in, pout_in, pco_in, pci_in, train, out,
     pin, pout, pco, pci, xa, xg, pa, pg, total, h1s, h1r, h2s, h2r, ds, dr, fs, fr, zs, zr, ag, xf, tr, wide, pi2, part, lr,
-    sw, sxa, sxg, str_, h1ss, h1rs, h2ss, h2rs, dss, drs, fss, frs, zss, zrs, azs, azr, y1s, y1r, y2s, y2r, lss, lrs,
+    sw, sxa, sxg, str_, h1ss, h1rs, h2ss, h2rs, dss, drs, fss, frs, zss, zrs, told_1, told_2, azs, azr, y1s, y1r, y2s, y2r, lss, lrs,
 ):
     ne = nz * NY
     half = nz // 2
@@ -101,9 +102,19 @@
     load_train.start()
 
     barrier = pltpu.get_barrier_semaphore()
-    greeted = [y_up, y_down, at(z, across)]
-    greeted += [at((z + step + nz) % nz, y) for step in (1, -1, 2, -2)]
-    greeted += [(ex, (layer + step) % nl) for step in range(1, nl)]
+    z_near = [at((z + step + nz) % nz, y) for step in (1, -1)]
+    if nl == 8:
+        x_near = [(ex, (layer + step) % nl) for step in (2, nl - 2)]
+        greeted = [y_up, y_down] + z_near + x_near + [(ex, layer + 1 - 2 * (layer % 2))]
+        tell_1, tell_2 = greeted[2:], x_near
+    else:
+        greeted = [y_up, y_down] + z_near + [(ex, (layer + step) % nl) for step in range(1, nl)]
+        tell_1, tell_2 = z_near, z_near
+
+    def tell(devices, sem):
+        for device in devices:
+            pl.semaphore_signal(sem, inc=1, device_id=device, device_id_type=MESH)
+
     for device in greeted:
         pl.semaphore_signal(barrier, inc=1, device_id=device, device_id_type=MESH)
 
@@ -249,6 +260,15 @@
         wide[j] = jnp.concatenate([first, second], axis=0).astype(jnp.bfloat16)
 
     def turn(i, _):
+        @pl.when(i == 3)
+        def _():
+            pl.semaphore_wait(told_1, len(tell_1))
+            tell(tell_2, told_2)
+
+        @pl.when(i == LAG2)
+        def _():
+            pl.semaphore_wait(told_2, len(tell_2))
+
         @pl.when((i > 0) & (i < last))
         def _():
             project(i, i)
@@ -292,6 +312,7 @@
     to_neighbour(1)
     pl.semaphore_wait(barrier, len(greeted))
     send_first_hop(0)
+    tell(tell_1, told_1)
     neighbour(0).start()
     neighbour(1).start()
     load_train.wait()
@@ -338,25 +359,12 @@
         remote(ag.at[e], ag.at[e], y1s, y1r.at[t, way], (y_up, y_down)[way]).wait_recv()
         return e
 
-    def gy2(t, way):
-        e = away(t) * NY + (down, up)[way]
-        rows = pl.ds(way * (R // 2), R // 2)
-        return remote(
-            ag.at[e, rows], ag.at[e, rows], y2s, y2r.at[t, way], (y_up, y_down)[way]
-        )
-
-    def gy2_wait(t):
-        e = away(t) * NY + across
-        for way in range(2):
-            rows = pl.ds(way * (R // 2), R // 2)
-            remote(
-                ag.at[e, rows], ag.at[e, rows], y2s, y2r.at[t, way], (y_up, y_down)[way]
-            ).wait_recv()
-        return e
-
-    for d in [hub, hub + 1] + list(range(hub - 1, 0, -1)):
+    direct = hub + XD
+    for d in [hub] + list(range(hub + 1, direct + 1)) + list(range(hub - 1, 0, -1)):
         gz(0, 2 * d - 1, d).start()
         gz(0, 2 * d, -d).start()
+    own_across = remote(ag.at[ex], ag.at[ex], y2s, y2r.at[0, 0], at(z, across))
+    own_across.start()
     gy1(0, 0).start()
     gy1(0, 1).start()
 
@@ -364,11 +372,11 @@
     for sent, sem in ((h1s, h1ss), (h2s, h2ss), (ds, dss), (fs, fss), (zs, zss)):
         remote(sent, sent, sem, azr.at[0], y_up).wait_send()
 
-    first = 2 * (hub + 1) + 1
+    first = 2 * direct + 1
 
     def chunk(n):
         pair, side = (n - 1) // 2, (n - 1) % 2
-        early = 2 * jnp.where(pair < hub, hub - pair, hub + 1) - 1 + side
+        early = 2 * jnp.where(pair < hub, hub - pair, pair + 1) - 1 + side
         m = n - first - 1
         late = jnp.where(n == first, nz - 1, nz - 3 - 2 * (m // 2) + (m + 2) % 2)
         return jnp.where(n == 0, 0, jnp.where(n < first, early, late))
@@ -377,10 +385,10 @@
         gz(t, t, 1).wait_recv()
 
     arrived(2 * hub - 1)
-    for d in range(half, hub + 1, -1):
+    for d in range(half, direct, -1):
         gz(2 * hub - 1, 2 * d - 1, d - hub).start()
     arrived(2 * hub)
-    for d in range(half - 1, hub + 1, -1):
+    for d in range(half - 1, direct, -1):
         gz(2 * hub, 2 * d, hub - d).start()
 
     def forward(n, _):
@@ -390,16 +398,9 @@
         def _():
             arrived(t)
 
+        gy3(t, y).start()
         gy1(t, 0).start()
         gy1(t, 1).start()
-        return 0
-
-    def forward_half(n, _):
-        t = chunk(n)
-        gy1_wait(t, 0)
-        gy2(t, 0).start()
-        gy1_wait(t, 1)
-        gy2(t, 1).start()
         return 0
 
     def gy3(t, yy):
@@ -412,18 +413,6 @@
         gy3(t, y).start()
         gy1(t, 0).start()
         gy1(t, 1).start()
-        return 0
-
-    def spread_three(n, _):
-        t = chunk(n)
-        for yy in (y, down, up):
-            e = away(t) * NY + yy
-            spread(e, ag[e])
-        return 0
-
-    def spread_last(n, _):
-        e = gy2_wait(chunk(n))
-        spread(e, ag[e])
         return 0
 
     def spread_late(n, _):
@@ -439,10 +428,8 @@
         return 0
 
     lax.fori_loop(1, first, forward, 0)
-    lax.fori_loop(0, first, forward_half, 0)
     lax.fori_loop(first, nz, forward_late, 0)
-    lax.fori_loop(0, first, spread_three, 0)
-    lax.fori_loop(0, first, spread_last, 0)
+    lax.fori_loop(0, first, spread_late, 0)
     lax.fori_loop(first, nz, spread_late, 0)
 
     def score(j, acc):
@@ -518,7 +505,7 @@
             pltpu.VMEM((nl - 1, rows, T), f32),
             dma((4,)), dma((nz,)), dma((nz,)), dma,
             dma, dma((nz, 2)), dma, dma((nz, 2)), dma, dma((ND,)), dma, dma((2,)),
-            dma, dma((nz + 1, 2)),
+            dma, dma((nz + 1, 2)), pltpu.SemaphoreType.REGULAR, pltpu.SemaphoreType.REGULAR,
             dma, dma((nz,)), dma, dma((nz, 2)), dma, dma((nz, 2)),
             dma, dma((nl - 1,)),
         ],

time: 68.5 us -> 67.7 us (0.988)
  Pallas kernels: 67 us -> 66.2 us
    pallas_call x1, Pallas kernels: 67 us -> 66.2 us  [on_device(): pl.pallas_call(functools.partial(kernel, nz, nl), out_shape=jax.ShapeDtyp...]
where the time goes in v5:
time: 67.7 us; the launch traced here: 67.5 us
  Pallas kernels  66.2 us (98%)
  local copies, waits for them, and re-layouts  1.35 us (2%)
    pallas_call x1, Pallas kernels, on_device(): pl.pallas_call(functools.partial(kernel, nz, nl), out_shape=jax.ShapeDtyp...  66.2 us

profile of v5, /device:TPU:1, one launch (start us, length us, event | category | flops | bytes accessed | tf_op | source)
XLA Modules:
  0.0 67.5 jit_solution(11853206964529750144)
XLA Ops:
  0.0 66.2 %shard_map.73 = f32[8,128]{1,0:T(8,128)} custom-call(bf16[1,224,8192]{2,1,0:T(8,128)(2,1)} %acts.1, bf16[1,64,8192]{2,1,0:T(8,128)(2,1)} %grads.1, bf16[1,64,224]{2,1,0:T(8,128)(2,1)} %pin_in.1, bf16[1,64,64]{2,1,0:T(8,128)(2,1)} %pout_in.1, f32[1,64,64]{2,1,0:T(8,128)} %pco_in.1, f32[1,64,64]{2,1,0:T(8,128)} %pci_in.1, bf16[1,32,4096]{2,1,0:T(8,128)(2,1)} %train.1), custom_call_target="tpu_custom_call" | custom-call | tf_op jit(solution)/shard_map/pallas_call | solution.py:474
  66.2 1.3 %reshape.3 = f32[16,32]{1,0:T(8,128)} reshape(f32[8,64]{1,0:T(8,128)} %bitcast.1) | data formatting | bytes 4096 | tf_op jit(solution)/shard_map/reshape | solution.py:516
